TPU v7x, 32 devices: a whole 2x2x4 slice. The times are simulated.
32 devices in a mesh: group: 2 (over x), pos: 16 (over z, y, core).
Axes of the slice: x: 2, y: 2, z: 4, core: 2. Of those that a mesh axis runs over, the one named last changes fastest.
Arguments:
- acts: bfloat16 [4, 1024, 1536], P('group', 'pos'), parts along dimension 0, may hold values from -12 to 12
- skips: bfloat16 [4, 2048, 1280], P('group', 'pos'), parts along dimension 0, may hold values from -6 to 6
- norm_gain: float32 [1536], replicated, may hold values from 0.6 to 1.6
- w_query: bfloat16 [1536, 256], replicated, may hold values from -4 to 4
- w_key: bfloat16 [1536, 256], replicated, may hold values from -4 to 4
- w_value: bfloat16 [1536, 768], replicated, may hold values from -0.15625 to 0.15625
- w_out: bfloat16 [768, 1536], replicated, may hold values from -0.21875 to 0.21875
- w_lift: bfloat16 [1536, 1536], P('pos'), may hold values from -0.15625 to 0.15625
- w_skip: bfloat16 [1280, 1536], P('pos'), may hold values from -0.15625 to 0.15625
- depth_kernel: float32 [3, 1536], replicated, may hold values from -3 to 3
- w_point: bfloat16 [1536, 1536], P(None, 'pos'), may hold values from -0.15625 to 0.15625
Outputs:
- decoded: bfloat16 [4, 2048, 1536], P('group', 'pos'), parts along dimension 0
There are 2 independent parts, one for each index of `group`. A program takes and returns all parts, laid end to end along the dimension named above; an argument that names none is the same for every part. Nothing has to cross between parts.
All inputs are finite; a program needn't handle non-finite values.
Results may differ from a plain program's by a relative error of at most 0.014.
Values may be sent and summed in bfloat16 or wider, within the bound.
A program may use at most 128 MiB of HBM per device.

v0:
```python
import jax
import jax.numpy as jnp
from jax import lax
from jax.sharding import PartitionSpec as P

HEADS = 4
HK = 64
HV = 192


def extended(cells, sides, width):
    for axis, dim in sides:
        count = lax.axis_size(axis)
        ends = count - 1
        head = lax.slice_in_dim(cells, 0, width, axis=dim)
        tail = lax.slice_in_dim(cells, cells.shape[dim] - width, cells.shape[dim], axis=dim)
        cells = jnp.concatenate(
            [
                lax.ppermute(tail, axis, [(i, (i + 1) % count) for i in range(ends)]),
                cells,
                lax.ppermute(head, axis, [((i + 1) % count, i) for i in range(ends)]),
            ],
            axis=dim,
        )
    return cells


def on_device(
    acts, skips, norm_gain, w_query, w_key, w_value, w_out, w_lift, w_skip, depth_kernel, w_point
):
    lift_full, skip_full, point_full = (
        lax.all_gather(w_lift, "pos", axis=0, tiled=True),
        lax.all_gather(w_skip, "pos", axis=0, tiled=True),
        lax.all_gather(w_point, "pos", axis=1, tiled=True),
    )
    seq_count, bin_rows, width = acts.shape
    actsf = acts.astype(jnp.float32)
    centre = actsf - jnp.mean(actsf, axis=-1, keepdims=True)
    normed = (
        centre * lax.rsqrt(jnp.mean(centre * centre, axis=-1, keepdims=True) + 1e-05) * norm_gain
    ).astype(jnp.bfloat16)
    flat = normed.reshape(seq_count * bin_rows, width)
    queries = (
        (jnp.dot(flat, w_query, preferred_element_type=jnp.float32) * HK ** (-0.5))
        .astype(jnp.bfloat16)
        .reshape(seq_count, bin_rows, HEADS, HK)
    )
    keys_here = (
        jnp.dot(flat, w_key, preferred_element_type=jnp.float32)
        .astype(jnp.bfloat16)
        .reshape(seq_count, bin_rows, HEADS * HK)
    )
    values_here = (
        jnp.dot(flat, w_value, preferred_element_type=jnp.float32)
        .astype(jnp.bfloat16)
        .reshape(seq_count, bin_rows, HEADS * HV)
    )
    running = jnp.full((seq_count, HEADS, bin_rows), -1e30, jnp.float32)
    key_piece = lax.all_gather(keys_here, "pos", axis=1, tiled=True)
    value_piece = lax.all_gather(values_here, "pos", axis=1, tiled=True)
    count = key_piece.shape[1]
    keyed = key_piece.reshape(seq_count, count, HEADS, HK)
    valued = value_piece.reshape(seq_count, count, HEADS, HV)
    scores = jnp.einsum("sqhd,skhd->shqk", queries, keyed, preferred_element_type=jnp.float32)
    newest = jnp.maximum(running, jnp.max(scores, axis=-1))
    weights = jnp.exp(scores - newest[..., None])
    totals = jnp.sum(weights, axis=-1)
    summed = jnp.einsum(
        "shqk,skhv->shqv", weights.astype(jnp.bfloat16), valued, preferred_element_type=jnp.float32
    )
    running, totals, summed = (newest, totals, summed)
    mixed = (
        (summed / totals[..., None])
        .transpose(0, 2, 1, 3)
        .reshape(seq_count * bin_rows, HEADS * HV)
        .astype(jnp.bfloat16)
    )
    attended = (
        actsf.reshape(seq_count * bin_rows, width)
        + jnp.dot(mixed, w_out, preferred_element_type=jnp.float32)
    ).astype(jnp.bfloat16)
    activated = jax.nn.gelu(attended.astype(jnp.float32)).astype(jnp.bfloat16)
    lifted = jnp.dot(activated, lift_full, preferred_element_type=jnp.float32)
    lifted = lifted.astype(jnp.bfloat16).reshape(seq_count, bin_rows, width)
    raised = jnp.repeat(lifted, 2, axis=1).reshape(seq_count * 2 * bin_rows, width)
    skip_act = (
        jax.nn.gelu(skips.astype(jnp.float32))
        .astype(jnp.bfloat16)
        .reshape(seq_count * 2 * bin_rows, skips.shape[2])
    )
    skip_term = jnp.dot(skip_act, skip_full, preferred_element_type=jnp.float32)
    merged = (
        (raised.astype(jnp.float32) + skip_term)
        .astype(jnp.bfloat16)
        .reshape(seq_count, 2 * bin_rows, width)
    )
    padded = extended(merged, (("pos", 1),), 1)
    paddedf = padded.astype(jnp.float32)
    spread = (
        depth_kernel[0] * paddedf[:, :-2]
        + depth_kernel[1] * paddedf[:, 1:-1]
        + depth_kernel[2] * paddedf[:, 2:]
    ).astype(jnp.bfloat16)
    spread = spread.reshape(seq_count * 2 * bin_rows, width)
    decoded = jnp.dot(spread, point_full, preferred_element_type=jnp.float32)
    return decoded.astype(jnp.bfloat16).reshape(seq_count, 2 * bin_rows, width)


def solution(mesh):
    return jax.shard_map(
        on_device,
        mesh=mesh,
        in_specs=(
            P("group", "pos", None),
            P("group", "pos", None),
            P(),
            P(),
            P(),
            P(),
            P(),
            P("pos", None),
            P("pos", None),
            P(),
            P(None, "pos"),
        ),
        out_specs=P("group", "pos", None),
        check_vma=False,
    )
```

profile of v0, /device:TPU:0, one launch (start us, length us, event | category | flops | bytes accessed | tf_op | source)
XLA Modules:
  0.0 268.4 jit_solution(8063212985456525454)
XLA Ops:
  6.5 0.0 copy-start
  6.5 0.0 copy-start.3
  6.5 0.0 all-gather.6.cloned.1.call-start
  6.5 1.3 convert_reduce_fusion
  7.8 1.3 multiply_reduce_fusion
  9.1 1.3 multiply_convert_fusion
  10.4 0.0 copy-done.3
  10.4 0.9 convolution_convert_fusion.3
  11.3 0.0 all-gather.6.cloned.1.call-update
  11.3 0.0 copy-start.4
  11.3 0.0 all-gather.8.cloned.1.call-start
  11.4 2.9 %convolution_convert_fusion.2 = bf16[128,768]{1,0:T(8,128)(2,1)} fusion(bf16[128,1536]{1,0:T(8,128)(2,1)S(1)} %bitcast.36, bf16[1536,768]{1,0:T(8,128)(2,1)} %param.16), kind=kOutput, calls=%fused_computation.30 | convolution fusion | flops 302088192 | bytes 2949120 | tf_op jit(solution)/shard_map/dot_general | solution.py:54
  14.3 0.0 all-gather.8.cloned.1.call-update
  14.3 0.0 all-gather.10.cloned.1.call-start
  14.3 0.7 all-gather.10.cloned.1.call-update
  15.0 0.0 all-gather.12.cloned.1.call-start
  15.1 0.5 all-gather.12.cloned.1.call-update
  15.6 0.0 all-gather.14.cloned.1.call-start
  15.6 0.5 all-gather.14.cloned.1.call-update
  16.2 0.0 copy-done.4
  16.2 0.9 fusion.16
  17.1 1.0 reshape.61
  18.1 2.4 fusion.13
  20.4 31.7 %all-gather.6.cloned.1.call-done = bf16[2,1024,256]{2,1,0:T(8,128)(2,1)} async-done(((bf16[2,64,256]{2,1,0:T(8,128)(2,1)}), bf16[2,1024,256]{2,1,0:T(8,128)(2,1)}) %all-gather.6.cloned.1.call-update) | async-done | bytes 1048592 | tf_op jit(solution)/shard_map/all_gather | solution.py:59
  52.1 1.5 copy.15
  53.6 0.5 fusion.38
  54.1 0.0 copy-start.1
  54.1 1.3 copy-done.1
  55.5 0.5 fusion.3
  56.0 42.6 %all-gather.8.cloned.1.call-done = bf16[2,1024,768]{2,1,0:T(8,128)(2,1)} async-done(((bf16[2,64,768]{2,1,0:T(8,128)(2,1)}), bf16[2,1024,768]{2,1,0:T(8,128)(2,1)}) %all-gather.8.cloned.1.call-update) | async-done | bytes 3145744 | tf_op jit(solution)/shard_map/all_gather | solution.py:60
  98.6 4.6 %copy.17 = bf16[2,1024,768]{1,2,0:T(8,128)(2,1)} copy(bf16[2,1024,768]{2,1,0:T(8,128)(2,1)} %all-gather.8.cloned.1.call-done) | data formatting | bytes 6291456 | tf_op jit(solution)/shard_map/all_gather | solution.py:60
  103.2 0.0 copy-start.2
  103.2 3.7 %fusion.15 = bf16[2,64,4,192]{3,1,2,0:T(8,128)(2,1)S(1)} fusion(bf16[2,1024,4,192]{1,3,2,0:T(8,128)(2,1)} %bitcast.40, f32[2,4,64,1024]{3,2,1,0:T(8,128)} %copy-done.1, f32[2,4,64]{2,1,0:T(4,128)S(1)} %broadcast_maximum_fusion, f32[2,64,4]{1,2,0:T(4,128)S(1)} %bitcast.48), kind=kOutput, calls=%fused_computation.28 | convolution fusion | flops 202571776 | bytes 5443584 | tf_op jit(solution)/shard_map/shqk,skhv->shqv/dot_general | solution.py:68
  106.9 0.2 copy.18
  107.2 0.2 convert_element_type.71
  107.4 45.7 %all-gather.10.cloned.1.call-done = bf16[1536,1536]{1,0:T(8,128)(2,1)} async-done(((bf16[96,1536]{1,0:T(8,128)(2,1)}), bf16[1536,1536]{1,0:T(8,128)(2,1)}) %all-gather.10.cloned.1.call-update) | async-done | bytes 4718608 | tf_op jit(solution)/shard_map/all_gather | solution.py:32
  153.1 0.0 copy-done
  153.1 0.0 copy-done.2
  153.1 3.7 %convolution_convert_fusion.1 = bf16[128,1536]{1,0:T(8,128)(2,1)S(1)} fusion(bf16[1536,1536]{1,0:T(8,128)(2,1)} %all-gather.10.cloned.1.call-done, bf16[128,768]{1,0:T(8,128)(2,1)S(1)} %convert_element_type.71, bf16[768,1536]{1,0:T(8,128)(2,1)S(1)} %copy-done, bf16[128,1536]{1,0:T(8,128)(2,1)S(1)} %bitcast.39), kind=kOutput, calls=%fused_computation.6 | convolution fusion | flops 908722176 | bytes 8060928 | tf_op jit(solution)/shard_map/dot_general | solution.py:83
  156.8 1.6 broadcast_in_dim.5
  158.3 0.0 copy-start.5
  158.3 3.2 %convert_element_type.78 = f32[256,1536]{1,0:T(8,128)} reshape(f32[2,64,2,1536]{3,2,1,0:T(2,128)} %broadcast_in_dim.5) | data formatting | bytes 3145728 | tf_op jit(solution)/shard_map/convert_element_type | solution.py:93
  161.5 41.0 %all-gather.12.cloned.1.call-done = bf16[1280,1536]{1,0:T(8,128)(2,1)} async-done(((bf16[80,1536]{1,0:T(8,128)(2,1)}), bf16[1280,1536]{1,0:T(8,128)(2,1)}) %all-gather.12.cloned.1.call-update) | async-done | bytes 3932176 | tf_op jit(solution)/shard_map/all_gather | solution.py:33
  202.6 0.0 copy-done.5
  202.6 0.0 copy-start.6
  202.6 3.8 %fusion = bf16[256,1536]{1,0:T(8,128)(2,1)S(1)} fusion(f32[256,1536]{1,0:T(8,128)} %convert_element_type.78, bf16[256,1280]{1,0:T(8,128)(2,1)S(1)} %bitcast.45, bf16[1280,1536]{1,0:T(8,128)(2,1)} %all-gather.12.cloned.1.call-done), kind=kOutput, calls=%fused_computation.1 | convolution fusion | flops 1007419392 | bytes 6946816 | tf_op jit(solution)/shard_map/dot_general | solution.py:91
  206.4 2.2 collective-permute-start
  208.6 1.3 collective-permute-start.1
  209.9 0.0 copy-done.6
  209.9 0.1 slice_reduce_fusion.2
  209.9 0.0 collective-permute-done
  210.0 1.7 collective-permute-done.1
  211.7 0.2 maximum_convert_fusion
  211.9 0.5 fusion.6
  212.4 44.8 %all-gather.14.cloned.1.call-done = bf16[1536,1536]{0,1:T(8,128)(2,1)} async-done(((bf16[1536,96]{0,1:T(8,128)(2,1)}), bf16[1536,1536]{0,1:T(8,128)(2,1)}) %all-gather.14.cloned.1.call-update) | async-done | bytes 4718608 | tf_op jit(solution)/shard_map/all_gather | solution.py:34
  257.2 4.6 %convolution_convert_fusion = bf16[256,1536]{1,0:T(8,128)(2,1)} fusion(bf16[256,1536]{1,0:T(8,128)(2,1)S(1)} %bitcast.44, bf16[1536,1536]{0,1:T(8,128)(2,1)} %all-gather.14.cloned.1.call-done), kind=kOutput, calls=%fused_computation.2 | convolution fusion | flops 1208352768 | bytes 6291456 | tf_op jit(solution)/shard_map/dot_general | solution.py:105
  (4 shorter events, 0.0 us)
Async XLA Ops:
  6.5 146.6 %copy-start = (bf16[768,1536]{1,0:T(8,128)(2,1)S(1)}, bf16[768,1536]{1,0:T(8,128)(2,1)}, u32[]{:S(2)}) copy-start(bf16[768,1536]{1,0:T(8,128)(2,1)} %param.17) | copy-start | bytes 7077892
  6.5 3.8 %copy-start.3 = (bf16[1536,256]{1,0:T(8,128)(2,1)S(1)}, bf16[1536,256]{1,0:T(8,128)(2,1)}, u32[]{:S(2)}) copy-start(bf16[1536,256]{1,0:T(8,128)(2,1)} %param.15) | copy-start | bytes 2359300
  6.5 45.6 %all-gather.6.cloned.1.call-start = ((), (), s32[]{:S(2)}) async-start(), calls=%async_computation | async-start | bytes 1114112 | tf_op jit(solution)/shard_map/all_gather | solution.py:59
  11.3 4.9 %copy-start.4 = (bf16[1536,256]{1,0:T(8,128)(2,1)S(1)}, bf16[1536,256]{1,0:T(8,128)(2,1)}, u32[]{:S(2)}) copy-start(bf16[1536,256]{1,0:T(8,128)(2,1)} %param.14) | copy-start | bytes 2359300
  11.3 87.3 %all-gather.8.cloned.1.call-start = ((), (), s32[]{:S(2)}) async-start(), calls=%async_computation.1 | async-start | bytes 3342336 | tf_op jit(solution)/shard_map/all_gather | solution.py:60
  14.3 138.8 %all-gather.10.cloned.1.call-start = ((), (), s32[]{:S(2)}) async-start(), calls=%async_computation.2 | async-start | bytes 5013504 | tf_op jit(solution)/shard_map/all_gather | solution.py:32
  15.0 187.6 %all-gather.12.cloned.1.call-start = ((), (), s32[]{:S(2)}) async-start(), calls=%async_computation.3 | async-start | bytes 4177920 | tf_op jit(solution)/shard_map/all_gather | solution.py:33
  15.6 241.7 %all-gather.14.cloned.1.call-start = ((), (), s32[]{:S(2)}) async-start(), calls=%async_computation.4 | async-start | bytes 5013504 | tf_op jit(solution)/shard_map/all_gather | solution.py:34
  54.1 1.4 copy-start.1
  103.2 49.9 %copy-start.2 = (bf16[2,64,1536]{2,1,0:T(8,128)(2,1)S(1)}, bf16[2,64,1536]{2,1,0:T(8,128)(2,1)}, u32[]{:S(2)}) copy-start(bf16[2,64,1536]{2,1,0:T(8,128)(2,1)} %param.11) | copy-start | bytes 1179652
  158.3 44.3 %copy-start.5 = (bf16[2,128,1280]{2,1,0:T(8,128)(2,1)S(1)}, bf16[2,128,1280]{2,1,0:T(8,128)(2,1)}, u32[]{:S(2)}) copy-start(bf16[2,128,1280]{2,1,0:T(8,128)(2,1)} %fusion.13) | copy-start | bytes 1966084
  202.6 7.3 %copy-start.6 = (f32[3,1536]{1,0:T(4,128)S(1)}, f32[3,1536]{1,0:T(4,128)}, u32[]{:S(2)}) copy-start(f32[3,1536]{1,0:T(4,128)} %param.20) | copy-start | bytes 55300
  206.4 3.5 %collective-permute-start = (bf16[2,1,1536]{2,1,0:T(2,128)(2,1)S(1)}, bf16[2,1,1536]{2,1,0:T(2,128)(2,1)S(1)}, u32[]{:S(2)}, u32[]{:S(2)}) collective-permute-start(bf16[2,1,1536]{2,1,0:T(2,128)(2,1)S(1)} %get-tuple-element.8), channel_id=1, source_target_pairs={{0,1},{1,2},{2,3},{3,4},{4,5},{5,6},{6,7},{7,8},{8,9},{9,10},{10,1... | collective-permute-start | bytes 18440 | tf_op jit(solution)/shard_map/ppermute | solution.py:19
  208.6 3.1 %collective-permute-start.1 = (bf16[2,1,1536]{2,1,0:T(2,128)(2,1)S(1)}, bf16[2,1,1536]{2,1,0:T(2,128)(2,1)S(1)}, u32[]{:S(2)}, u32[]{:S(2)}) collective-permute-start(bf16[2,1,1536]{2,1,0:T(2,128)(2,1)S(1)} %get-tuple-element.9), channel_id=1, source_target_pairs={{1,0},{2,1},{3,2},{4,3},{5,4},{6,5},{7,6},{8,7},{9,8},{10,9},{11,1... | collective-permute-start | bytes 18440 | tf_op jit(solution)/shard_map/ppermute | solution.py:21
Sparse Core Ops, SparseCore 0:
  11.4 40.6 all-gather.5
  54.4 44.1 all-gather.7
  100.9 52.1 all-gather.9
  155.2 47.3 all-gather.11
  204.7 52.4 all-gather.13
where the time goes:
time: 269 us; the launch traced here: 268 us
  waiting for transfers between devices  209 us (78%)
  matrix products  21 us (8%)
  local copies, waits for them, and re-layouts  13.7 us (5%)
  between operations  13.3 us (5%)
  other arithmetic  7.44 us (3%)
  starting transfers between devices  3.61 us (1%)
    all_gather x1, waiting for transfers between devices, on_device(): lax.all_gather(w_lift, 'pos', axis=0, tiled=True)  45.7 us
    all_gather x1, waiting for transfers between devices, on_device(): lax.all_gather(w_point, 'pos', axis=1, tiled=True)  44.8 us
    all_gather x1, waiting for transfers between devices, on_device(): value_piece = lax.all_gather(values_here, 'pos', axis=1, tiled=True)  42.6 us
    all_gather x1, waiting for transfers between devices, on_device(): lax.all_gather(w_skip, 'pos', axis=0, tiled=True)  41 us
    all_gather x1, waiting for transfers between devices, on_device(): key_piece = lax.all_gather(keys_here, 'pos', axis=1, tiled=True)  31.7 us
  transfers between devices with their start and end apart: 7, of which 6 were waited for; matrix products, arithmetic and copies ran while one was open for 12% of the time, Pallas kernels for 0%

commit v1 on v0

--- a/solution.py
+++ b/solution.py
@@ -1,6 +1,10 @@
+import functools
+
 import jax
 import jax.numpy as jnp
 from jax import lax
+from jax.experimental import pallas as pl
+from jax.experimental.pallas import tpu as pltpu
 from jax.sharding import PartitionSpec as P
 
 HEADS = 4
@@ -106,23 +110,384 @@
     return decoded.astype(jnp.bfloat16).reshape(seq_count, 2 * bin_rows, width)
 
 
+SEND_RING, SEND_SIDE, SEND_CROSS = 0, 1, 2
+KV, SKIP, MINE, THEIRS = 0, 1, 2, 3
+MESH = pl.DeviceIdType.MESH
+
+
+def fused_kernel(
+    groups, places,
+    acts_h, skips_h, gain_ref, wq_h, wk_h, wv_h, wo_h, lift_h, point_h, skip_h, depth_ref,
+    out_ref,
+    acts, skips, wq, wk, wv, wo, pair, skip_full, kv, normed, queries, mixed, activated,
+    skip_act, term, spread, halo_out, halo_in,
+    local_sem, send_sem, recv_sem, halo_send, halo_recv,
+):
+    chips = places // 2
+    reach = chips // 2
+    me, group = lax.axis_index("pos"), lax.axis_index("group")
+    core, chip = lax.rem(me, 2), lax.div(me, 2)
+    column, level = lax.rem(chip, 2), lax.div(chip, 2)
+    ring = level + column * (chips - 1 - 2 * level)
+    mine = lax.rem(group, 2)
+    partner = group + 1 - 2 * mine
+    side = chip * 2 + 1 - core
+    width = acts.shape[1]
+    skip_rows, pair_rows, bins = skip_h.shape[0], lift_h.shape[0], acts.shape[0] // 2
+
+    def chip_at(place):
+        place = lax.rem(place + chips, chips)
+        far = lax.div(place, reach)
+        return (1 - far) * 2 * place + far * (2 * (chips - 1 - place) + 1)
+
+    right, left = chip_at(ring + 1) * 2 + core, chip_at(ring - 1) * 2 + core
+
+    def origin(way, hops, of_core):
+        return chip_at(ring - hops if way == 0 else ring + hops) * 2 + of_core
+
+    def view(array, device, part):
+        if array == KV:
+            if part is None:
+                return kv.at[device]
+            return kv.at[device, pl.ds(part * bins, bins)]
+        rows = skip_rows if array == SKIP else pair_rows
+        first = (rows // 2 + 15) // 16 * 16
+        start, size = ((0, rows), (0, first), (first, rows - first))[0 if part is None else part + 1]
+        window = pl.ds(pl.multiple_of(device * rows + start, 16), size)
+        if array == SKIP:
+            return skip_full.at[window]
+        return pair.at[mine if array == MINE else 1 - mine, window]
+
+    def slot(way, hops):
+        return way * reach + hops - 1
+
+    def part_of(way, hops):
+        return way if hops == reach else None
+
+    own_slot = 2 * reach
+    sent = []
+
+    def send(array, ref, kind, index, target, at_array=None):
+        at_array = array if at_array is None else at_array
+        copy = pltpu.make_async_remote_copy(
+            src_ref=ref,
+            dst_ref=ref,
+            send_sem=send_sem.at[array, kind, index],
+            recv_sem=recv_sem.at[at_array, 1 if kind == SEND_SIDE else 0, index],
+            device_id=target,
+            device_id_type=MESH,
+        )
+        copy.start()
+        sent.append(copy)
+
+    def arrived(array, plane, index, ref):
+        pltpu.make_async_remote_copy(
+            src_ref=ref,
+            dst_ref=ref,
+            send_sem=send_sem.at[array, 0, index],
+            recv_sem=recv_sem.at[array, plane, index],
+            device_id={"pos": side},
+            device_id_type=MESH,
+        ).wait_recv()
+
+    def onward(array, way, hops):
+        if hops < reach:
+            ref = view(array, origin(way, hops, core), part_of(way, hops + 1))
+            send(array, ref, SEND_RING, slot(way, hops + 1), {"pos": right if way == 0 else left})
+
+    def pump(array, hops):
+        for way in (0, 1):
+            ref = view(array, origin(way, hops, core), part_of(way, hops))
+            arrived(array, 0, slot(way, hops), ref)
+            if array != THEIRS:
+                onward(array, way, hops)
+            if array == MINE:
+                send(array, ref, SEND_CROSS, slot(way, hops), {"group": partner}, THEIRS)
+            send(array, ref, SEND_SIDE, slot(way, hops), {"pos": side})
+
+    def begin(array):
+        if array != THEIRS:
+            onward(array, 0, 0)
+            onward(array, 1, 0)
+        send(array, view(array, me, None), SEND_SIDE, own_slot, {"pos": side})
+
+    def from_side(array):
+        arrived(array, 1, own_slot, view(array, side, None))
+        for hops in range(1, reach + 1):
+            for way in (0, 1):
+                ref = view(array, origin(way, hops, 1 - core), part_of(way, hops))
+                arrived(array, 1, slot(way, hops), ref)
+
+    def fetch(index, source, target):
+        copy = pltpu.make_async_copy(source, target, local_sem.at[index])
+        copy.start()
+        return copy
+
+    own_pair = pl.ds(pl.multiple_of(me * pair_rows, 16), pair_rows)
+    own_skip = pl.ds(pl.multiple_of(me * skip_rows, 16), skip_rows)
+    shards = [
+        fetch(0, lift_h, pair.at[0, own_pair]),
+        fetch(1, point_h, pair.at[1, own_pair]),
+        fetch(2, skip_h, skip_full.at[own_skip]),
+    ]
+    first_inputs = [fetch(3, acts_h, acts), fetch(4, wk_h, wk), fetch(5, wv_h, wv), fetch(6, wq_h, wq)]
+    later_inputs = [fetch(7, skips_h, skips), fetch(8, wo_h, wo)]
+
+    ahead, behind = lax.rem(me + 1, places), lax.rem(me + places - 1, places)
+    barrier = pltpu.get_barrier_semaphore()
+    for place in (left, right, side, ahead, behind):
+        pl.semaphore_signal(barrier, inc=1, device_id={"pos": place}, device_id_type=MESH)
+    pl.semaphore_signal(barrier, inc=1, device_id={"group": partner}, device_id_type=MESH)
+    pl.semaphore_wait(barrier, 6)
+
+    for copy in shards:
+        copy.wait()
+    begin(MINE)
+    begin(SKIP)
+    begin(THEIRS)
+
+    for copy in first_inputs:
+        copy.wait()
+    actsf = acts[...].astype(jnp.float32)
+    centre = actsf - jnp.mean(actsf, axis=-1, keepdims=True)
+    scale = lax.rsqrt(jnp.mean(centre * centre, axis=-1, keepdims=True) + 1e-05)
+    normed[...] = (centre * scale * gain_ref[...]).astype(jnp.bfloat16)
+    key_width = HEADS * HK
+
+    def dot(a, b):
+        return jnp.dot(a, b, preferred_element_type=jnp.float32)
+
+    def dot_t(a, b):
+        return lax.dot_general(a, b, (((1,), (1,)), ((), ())), preferred_element_type=jnp.float32)
+
+    kv[me, :, 0:key_width] = dot(normed[...], wk[...]).astype(jnp.bfloat16)
+    for tile in range(HEADS * HV // 256):
+        kv[me, :, key_width + tile * 256 : key_width + tile * 256 + 256] = dot(
+            normed[...], wv[:, tile * 256 : tile * 256 + 256]
+        ).astype(jnp.bfloat16)
+    begin(KV)
+    queries[...] = (dot(normed[...], wq[...]) * HK ** (-0.5)).astype(jnp.bfloat16)
+
+    for copy in later_inputs:
+        copy.wait()
+    pump(MINE, 1)
+    pump(SKIP, 1)
+    pump(KV, 1)
+
+    @pl.loop(0, skips.shape[0] // 64)
+    def _(step):
+        rows = pl.ds(pl.multiple_of(step * 64, 64), 64)
+        skip_act[rows] = jax.nn.gelu(skips[rows].astype(jnp.float32)).astype(jnp.bfloat16)
+
+    for hops in range(2, reach + 1):
+        pump(KV, hops)
+        pump(MINE, hops)
+        pump(SKIP, hops)
+        if hops < reach:
+            pump(THEIRS, hops - 1)
+    from_side(KV)
+
+    lane = lax.broadcasted_iota(jnp.int32, (bins, 2 * HK), 1)
+    wide_lane = lax.broadcasted_iota(jnp.int32, (bins, 2 * HV), 1)
+    keys_all = places * bins
+    for seq in range(2):
+        here = pl.ds(seq * bins, bins)
+        for two in range(HEADS // 2):
+            q = queries[here, two * 2 * HK : (two + 1) * 2 * HK]
+            zero = jnp.zeros_like(q)
+            both = jnp.concatenate([jnp.where(lane < HK, q, zero), jnp.where(lane < HK, zero, q)], axis=0)
+            k = kv[:, here, two * 2 * HK : (two + 1) * 2 * HK].reshape(keys_all, 2 * HK)
+            scores = dot_t(both, k)
+            weights = jnp.exp(scores - jnp.max(scores, axis=-1, keepdims=True))
+            totals = jnp.sum(weights, axis=-1, keepdims=True)
+            value_at = key_width + two * 2 * HV
+            v = kv[:, here, value_at : value_at + 2 * HV].reshape(keys_all, 2 * HV)
+            summed = dot(weights.astype(jnp.bfloat16), v) / totals
+            mixed[here, two * 2 * HV : (two + 1) * 2 * HV] = jnp.where(
+                wide_lane < HV, summed[:bins], summed[bins:]
+            ).astype(jnp.bfloat16)
+
+    tiles = width // 256
+
+    def tile_at(step):
+        return pl.ds(pl.multiple_of(step * 256, 256), 256)
+
+    @pl.loop(0, tiles)
+    def _(step):
+        cols = tile_at(step)
+        attended = (acts[:, cols].astype(jnp.float32) + dot(mixed[...], wo[:, cols])).astype(jnp.bfloat16)
+        activated[:, cols] = jax.nn.gelu(attended.astype(jnp.float32)).astype(jnp.bfloat16)
+
+    for hops in range(max(reach - 1, 1), reach):
+        pump(THEIRS, hops)
+    from_side(SKIP)
+
+    @pl.loop(0, tiles)
+    def _(step):
+        cols = tile_at(step)
+        term[:, cols] = dot(skip_act[...], skip_full[:, cols])
+
+    pump(THEIRS, reach)
+    from_side(MINE)
+    from_side(THEIRS)
+
+    halo_out[...] = jnp.zeros_like(halo_out)
+    ups = 2 * bins
+    twice = (
+        lax.div(lax.broadcasted_iota(jnp.int32, (2 * ups, 2 * bins), 0), 2)
+        == lax.broadcasted_iota(jnp.int32, (2 * ups, 2 * bins), 1)
+    ).astype(jnp.float32).astype(jnp.bfloat16)
+
+    @pl.loop(0, tiles)
+    def _(step):
+        cols = tile_at(step)
+        lifted = dot(activated[...], pair[0, :, cols]).astype(jnp.bfloat16)
+        merged = (dot(twice, lifted) + term[:, cols]).astype(jnp.bfloat16).astype(jnp.float32)
+        term[:, cols] = merged
+        for seq in range(2):
+            halo_out[0, seq : seq + 1, cols] = merged[seq * ups + ups - 1 : seq * ups + ups]
+            halo_out[1, seq : seq + 1, cols] = merged[seq * ups : seq * ups + 1]
+
+    edges = []
+    for way, place in ((0, ahead), (1, behind)):
+        copy = pltpu.make_async_remote_copy(
+            src_ref=halo_out.at[way],
+            dst_ref=halo_in.at[way],
+            send_sem=halo_send.at[way],
+            recv_sem=halo_recv.at[way],
+            device_id={"pos": place},
+            device_id_type=MESH,
+        )
+        copy.start()
+        edges.append(copy)
+    for copy in edges:
+        copy.wait()
+
+    row = lax.broadcasted_iota(jnp.int32, (ups, 256), 0)
+
+    @pl.loop(0, tiles)
+    def _(step):
+        cols = tile_at(step)
+        for seq in range(2):
+            rows = pl.ds(seq * ups, ups)
+            now = term[rows, cols]
+            before = jnp.where(me > 0, halo_in[0, seq : seq + 1, cols], 0.0)
+            after = jnp.where(me < places - 1, halo_in[1, seq : seq + 1, cols], 0.0)
+            prev = jnp.where(row == 0, before, pltpu.roll(now, 1, 0))
+            following = jnp.where(row == ups - 1, after, pltpu.roll(now, ups - 1, 0))
+            spread[rows, cols] = (
+                depth_ref[0:1, cols] * prev + depth_ref[1:2, cols] * now + depth_ref[2:3, cols] * following
+            ).astype(jnp.bfloat16)
+
+    @pl.loop(0, tiles)
+    def _(step):
+        cols = tile_at(step)
+        out_ref[:, cols] = dot_t(spread[...], pair[1, cols, :]).astype(jnp.bfloat16)
+
+    for copy in sent:
+        copy.wait_send()
+
+
+def fused(
+    groups, places,
+    acts, skips, norm_gain, w_query, w_key, w_value, w_out, w_lift, w_skip, depth_kernel, w_point
+):
+    seqs, bins, width = acts.shape
+    ups, channels = skips.shape[1:]
+    key_width, value_width = w_key.shape[1], w_value.shape[1]
+    reach = places // 4
+    slots = 2 * reach + 1
+    bf, f32 = jnp.bfloat16, jnp.float32
+    anywhere = pl.BlockSpec(memory_space=pl.ANY)
+    vmem = pl.BlockSpec(memory_space=pltpu.VMEM)
+    rows, up_rows = seqs * bins, seqs * ups
+    out = pl.pallas_call(
+        functools.partial(fused_kernel, groups, places),
+        out_shape=jax.ShapeDtypeStruct((up_rows, width), bf),
+        in_specs=[anywhere, anywhere, vmem] + [anywhere] * 7 + [vmem],
+        out_specs=vmem,
+        scratch_shapes=[
+            pltpu.VMEM((rows, width), bf),
+            pltpu.VMEM((up_rows, channels), bf),
+            pltpu.VMEM((width, key_width), bf),
+            pltpu.VMEM((width, key_width), bf),
+            pltpu.VMEM((width, value_width), bf),
+            pltpu.VMEM((value_width, width), bf),
+            pltpu.VMEM((2, width, width), bf),
+            pltpu.VMEM((channels, width), bf),
+            pltpu.VMEM((places, rows, key_width + value_width), bf),
+            pltpu.VMEM((rows, width), bf),
+            pltpu.VMEM((rows, key_width), bf),
+            pltpu.VMEM((rows, value_width), bf),
+            pltpu.VMEM((rows, width), bf),
+            pltpu.VMEM((up_rows, channels), bf),
+            pltpu.VMEM((up_rows, width), f32),
+            pltpu.VMEM((up_rows, width), bf),
+            pltpu.VMEM((2, 8, width), f32),
+            pltpu.VMEM((2, 8, width), f32),
+            pltpu.SemaphoreType.DMA((9,)),
+            pltpu.SemaphoreType.DMA((4, 3, slots)),
+            pltpu.SemaphoreType.DMA((4, 2, slots)),
+            pltpu.SemaphoreType.DMA((2,)),
+            pltpu.SemaphoreType.DMA((2,)),
+        ],
+        compiler_params=pltpu.CompilerParams(
+            collective_id=0, has_side_effects=True, vmem_limit_bytes=56 * 1024 * 1024
+        ),
+        cost_estimate=pl.CostEstimate(
+            flops=4 * 10**9, bytes_accessed=3 * 10**7, transcendentals=10**6
+        ),
+    )(
+        acts.reshape(rows, width),
+        skips.reshape(up_rows, channels),
+        norm_gain.reshape(1, width),
+        w_query,
+        w_key,
+        w_value,
+        w_out,
+        w_lift,
+        w_point.T,
+        w_skip,
+        depth_kernel,
+    )
+    return out.reshape(seqs, ups, width)
+
+
+def suits(mesh, shapes):
+    places, groups = mesh.shape["pos"], mesh.shape["group"]
+    lift, skip = shapes
+    return (
+        places % 4 == 0
+        and places <= 16
+        and groups % 2 == 0
+        and lift % places == 0
+        and skip % places == 0
+        and lift // places % 16 == 0
+        and skip // places % 16 == 0
+    )
+
+
 def solution(mesh):
-    return jax.shard_map(
-        on_device,
-        mesh=mesh,
-        in_specs=(
-            P("group", "pos", None),
-            P("group", "pos", None),
-            P(),
-            P(),
-            P(),
-            P(),
-            P(),
-            P("pos", None),
-            P("pos", None),
-            P(),
-            P(None, "pos"),
-        ),
-        out_specs=P("group", "pos", None),
-        check_vma=False,
-    )
+    specs = (
+        P("group", "pos", None),
+        P("group", "pos", None),
+        P(),
+        P(),
+        P(),
+        P(),
+        P(),
+        P("pos", None),
+        P("pos", None),
+        P(),
+        P(None, "pos"),
+    )
+
+    def run(*args):
+        body = on_device
+        if suits(mesh, (args[7].shape[0], args[8].shape[0])):
+            body = functools.partial(fused, mesh.shape["group"], mesh.shape["pos"])
+        return jax.shard_map(
+            body, mesh=mesh, in_specs=specs, out_specs=P("group", "pos", None), check_vma=False
+        )(*args)
+
+    return run

time: 269 us -> 92.8 us (0.34)
  waiting for transfers between devices: 209 us -> 0 us
  Pallas kernels: 0 us -> 89.2 us
  matrix products: 21 us -> 0 us
  between operations: 13.3 us -> 0.01 us
  local copies, waits for them, and re-layouts: 13.7 us -> 3.36 us
  other arithmetic: 7.44 us -> 0 us
  starting transfers between devices: 3.61 us -> 0 us
    all_gather x5 -> x0, waiting for transfers between devices: 206 us -> none  [the longest x1 45.7 us: on_device(): lax.all_gather(w_lift, 'pos', axis=0, tiled=True)]
    pallas_call x0 -> x1, Pallas kernels: none -> 89.2 us  [fused(): pl.pallas_call(functools.partial(fused_kernel, groups, places), out_shape...]
    dot_general x8 -> x0, matrix products: 21 us -> none  [the longest x1 4.63 us: on_device(): decoded = jnp.dot(spread, point_full, preferred_element_type=jnp.float32)]
    all_gather x2 -> x0, local copies, waits for them, and re-layouts: 6.13 us -> none  [the longest x1 4.65 us: on_device(): value_piece = lax.all_gather(values_here, 'pos', axis=1, tiled=True)]
    convert_element_type x4 -> x0, other arithmetic: 4.37 us -> none  [the longest x1 2.37 us: on_device(): skip_act = jax.nn.gelu(skips.astype(jnp.float32)).astype(jnp.bfloat16).re...]
    convert_element_type x3 -> x0, local copies, waits for them, and re-layouts: 3.65 us -> none  [the longest x1 3.21 us: on_device(): raised.astype(jnp.float32) + skip_term]
    ppermute x2 -> x0, starting transfers between devices: 3.45 us -> none  [the longest x1 2.16 us: extended(): lax.ppermute(tail, axis, [(i, (i + 1) % count) for i in range(ends)])]
    reduce_sum x3 -> x0, other arithmetic: 3.05 us -> none  [the longest x1 1.28 us: on_device(): centre = actsf - jnp.mean(actsf, axis=-1, keepdims=True)]
  transfers between devices with their start and end apart: 7 -> 0, of which waited for: 6 -> 0; matrix products, arithmetic and copies ran while one was open for 12% -> 0% of each run, Pallas kernels for 0% -> 0%
where the time goes in v1:
time: 92.8 us; the launch traced here: 92.6 us
  Pallas kernels  89.2 us (96%)
  local copies, waits for them, and re-layouts  3.36 us (4%)
    pallas_call x1, Pallas kernels, fused(): pl.pallas_call(functools.partial(fused_kernel, groups, places), out_shape...  89.2 us
    unnamed x1, local copies, waits for them, and re-layouts  2.06 us

profile of v1, /device:TPU:0, one launch (start us, length us, event | category | flops | bytes accessed | tf_op | source)
XLA Modules:
  0.0 92.6 jit_solution(15898385250117650215)
XLA Ops:
  0.0 1.3 %reshape.14.gain_ref = f32[1,1536]{1,0:T(1,128)} reshape(f32[1536]{0:T(1024)} %param.13) | data formatting | bytes 12288 | tf_op jit(solution)/shard_map/reshape | solution.py:443
  1.3 89.2 %shard_map.109 = bf16[256,1536]{1,0:T(8,128)(2,1)} custom-call(bf16[128,1536]{1,0:T(8,128)(2,1)} %bitcast.6, bf16[256,1280]{1,0:T(8,128)(2,1)} %bitcast.5, f32[1,1536]{1,0:T(1,128)} %reshape.14.gain_ref, bf16[1536,256]{1,0:T(8,128)(2,1)} %wq_h.1, bf16[1536,256]{1,0:T(8,128)(2,1)} %wk_h.1, bf16[1536,768]{1,0:T(8,128)(2,1)} %wv_h.1, bf16[768,1536]{1,0:T(8,128)(2,1)} %wo_h.1, ...), custom_call_target="tpu_custom_call" | custom-call | flops 4000000000 | bytes 30000000 | tf_op jit(solution)/shard_map/pallas_call | solution.py:404
  90.5 2.1 %copy.13 = bf16[2,128,1536]{2,1,0:T(8,128)(2,1)} copy(bf16[2,128,1536]{2,1,0:T(8,128)(2,1)} %bitcast.4) | data formatting | bytes 1572864

commit v2 on v1

--- a/solution.py
+++ b/solution.py
@@ -111,7 +111,10 @@
 
 
 SEND_RING, SEND_SIDE, SEND_CROSS = 0, 1, 2
-KV, SKIP, MINE, THEIRS = 0, 1, 2, 3
+KV, SKIP, SKIP_MINE, SKIP_THEIRS, LIFT_MINE, LIFT_THEIRS, POINT_MINE, POINT_THEIRS = range(8)
+MINE = (SKIP_MINE, LIFT_MINE, POINT_MINE)
+THEIRS = (SKIP_THEIRS, LIFT_THEIRS, POINT_THEIRS)
+ALONE = 16
 MESH = pl.DeviceIdType.MESH
 
 
@@ -150,13 +153,24 @@
             if part is None:
                 return kv.at[device]
             return kv.at[device, pl.ds(part * bins, bins)]
-        rows = skip_rows if array == SKIP else pair_rows
-        first = (rows // 2 + 15) // 16 * 16
+        owned = mine if array in MINE else 1 - mine
+        if array == SKIP:
+            at, rows, first = 2 * ALONE, skip_rows - 2 * ALONE, (skip_rows // 2 - ALONE) // 16 * 16
+        elif array in (SKIP_MINE, SKIP_THEIRS):
+            at, rows, first = owned * ALONE, ALONE, ALONE
+        else:
+            half = pair_rows // 2
+            low = half // 2 // 16 * 16
+            at, rows = owned * half, half
+            first = half - low if array in (LIFT_MINE, LIFT_THEIRS) else low
         start, size = ((0, rows), (0, first), (first, rows - first))[0 if part is None else part + 1]
-        window = pl.ds(pl.multiple_of(device * rows + start, 16), size)
-        if array == SKIP:
-            return skip_full.at[window]
-        return pair.at[mine if array == MINE else 1 - mine, window]
+        if array <= SKIP_THEIRS:
+            return skip_full.at[pl.ds(pl.multiple_of(device * skip_rows + at + start, 16), size)]
+        window = pl.ds(pl.multiple_of(device * pair_rows + at + start, 16), size)
+        return pair.at[0 if array in (LIFT_MINE, LIFT_THEIRS) else 1, window]
+
+    def absent(array, way, hops):
+        return array in (SKIP_MINE, SKIP_THEIRS) and hops == reach and way == 1
 
     def slot(way, hops):
         return way * reach + hops - 1
@@ -191,30 +205,36 @@
         ).wait_recv()
 
     def onward(array, way, hops):
-        if hops < reach:
+        if hops < reach and not absent(array, way, hops + 1):
             ref = view(array, origin(way, hops, core), part_of(way, hops + 1))
             send(array, ref, SEND_RING, slot(way, hops + 1), {"pos": right if way == 0 else left})
 
     def pump(array, hops):
         for way in (0, 1):
+            if absent(array, way, hops):
+                continue
             ref = view(array, origin(way, hops, core), part_of(way, hops))
             arrived(array, 0, slot(way, hops), ref)
-            if array != THEIRS:
+            if array not in THEIRS:
                 onward(array, way, hops)
-            if array == MINE:
-                send(array, ref, SEND_CROSS, slot(way, hops), {"group": partner}, THEIRS)
+            if array in MINE:
+                send(array, ref, SEND_CROSS, slot(way, hops), {"group": partner}, array + 1)
             send(array, ref, SEND_SIDE, slot(way, hops), {"pos": side})
 
     def begin(array):
-        if array != THEIRS:
+        if array not in THEIRS:
             onward(array, 0, 0)
             onward(array, 1, 0)
+
+    def begin_side(array):
         send(array, view(array, me, None), SEND_SIDE, own_slot, {"pos": side})
 
     def from_side(array):
         arrived(array, 1, own_slot, view(array, side, None))
         for hops in range(1, reach + 1):
             for way in (0, 1):
+                if absent(array, way, hops):
+                    continue
                 ref = view(array, origin(way, hops, 1 - core), part_of(way, hops))
                 arrived(array, 1, slot(way, hops), ref)
 
@@ -242,16 +262,17 @@
 
     for copy in shards:
         copy.wait()
-    begin(MINE)
-    begin(SKIP)
-    begin(THEIRS)
+    for array in (LIFT_MINE, SKIP_MINE, POINT_MINE, SKIP):
+        begin(array)
+    for array in range(SKIP, POINT_THEIRS + 1):
+        begin_side(array)
 
     for copy in first_inputs:
         copy.wait()
     actsf = acts[...].astype(jnp.float32)
     centre = actsf - jnp.mean(actsf, axis=-1, keepdims=True)
     scale = lax.rsqrt(jnp.mean(centre * centre, axis=-1, keepdims=True) + 1e-05)
-    normed[...] = (centre * scale * gain_ref[...]).astype(jnp.bfloat16)
+    normed[...] = (centre * scale * gain_ref[...].reshape(1, -1)).astype(jnp.bfloat16)
     key_width = HEADS * HK
 
     def dot(a, b):
@@ -266,13 +287,13 @@
             normed[...], wv[:, tile * 256 : tile * 256 + 256]
         ).astype(jnp.bfloat16)
     begin(KV)
+    begin_side(KV)
     queries[...] = (dot(normed[...], wq[...]) * HK ** (-0.5)).astype(jnp.bfloat16)
 
     for copy in later_inputs:
         copy.wait()
-    pump(MINE, 1)
-    pump(SKIP, 1)
-    pump(KV, 1)
+    for array in (LIFT_MINE, SKIP_MINE, POINT_MINE, SKIP, KV):
+        pump(array, 1)
 
     @pl.loop(0, skips.shape[0] // 64)
     def _(step):
@@ -280,11 +301,12 @@
         skip_act[rows] = jax.nn.gelu(skips[rows].astype(jnp.float32)).astype(jnp.bfloat16)
 
     for hops in range(2, reach + 1):
-        pump(KV, hops)
-        pump(MINE, hops)
-        pump(SKIP, hops)
+        order = (LIFT_MINE, SKIP_MINE, KV, POINT_MINE, SKIP)
+        for array in order if hops < reach else (KV, LIFT_MINE, SKIP_MINE, POINT_MINE, SKIP):
+            pump(array, hops)
         if hops < reach:
-            pump(THEIRS, hops - 1)
+            for array in THEIRS:
+                pump(array, hops - 1)
     from_side(KV)
 
     lane = lax.broadcasted_iota(jnp.int32, (bins, 2 * HK), 1)
@@ -319,17 +341,21 @@
         activated[:, cols] = jax.nn.gelu(attended.astype(jnp.float32)).astype(jnp.bfloat16)
 
     for hops in range(max(reach - 1, 1), reach):
-        pump(THEIRS, hops)
-    from_side(SKIP)
+        for array in THEIRS:
+            pump(array, hops)
+    pump(SKIP_THEIRS, reach)
+    pump(LIFT_THEIRS, reach)
+    for array in (SKIP, SKIP_MINE, SKIP_THEIRS):
+        from_side(array)
 
     @pl.loop(0, tiles)
     def _(step):
         cols = tile_at(step)
         term[:, cols] = dot(skip_act[...], skip_full[:, cols])
 
-    pump(THEIRS, reach)
-    from_side(MINE)
-    from_side(THEIRS)
+    pump(POINT_THEIRS, reach)
+    from_side(LIFT_MINE)
+    from_side(LIFT_THEIRS)
 
     halo_out[...] = jnp.zeros_like(halo_out)
     ups = 2 * bins
@@ -378,6 +404,9 @@
             spread[rows, cols] = (
                 depth_ref[0:1, cols] * prev + depth_ref[1:2, cols] * now + depth_ref[2:3, cols] * following
             ).astype(jnp.bfloat16)
+
+    from_side(POINT_MINE)
+    from_side(POINT_THEIRS)
 
     @pl.loop(0, tiles)
     def _(step):
@@ -426,8 +455,8 @@
             pltpu.VMEM((2, 8, width), f32),
             pltpu.VMEM((2, 8, width), f32),
             pltpu.SemaphoreType.DMA((9,)),
-            pltpu.SemaphoreType.DMA((4, 3, slots)),
-            pltpu.SemaphoreType.DMA((4, 2, slots)),
+            pltpu.SemaphoreType.DMA((8, 3, slots)),
+            pltpu.SemaphoreType.DMA((8, 2, slots)),
             pltpu.SemaphoreType.DMA((2,)),
             pltpu.SemaphoreType.DMA((2,)),
         ],
@@ -440,7 +469,7 @@
     )(
         acts.reshape(rows, width),
         skips.reshape(up_rows, channels),
-        norm_gain.reshape(1, width),
+        norm_gain,
         w_query,
         w_key,
         w_value,
@@ -464,6 +493,9 @@
         and skip % places == 0
         and lift // places % 16 == 0
         and skip // places % 16 == 0
+        and skip // places >= 64
+        and lift // places % 32 == 0
+        and lift // places >= 64
     )
 
 

time: 92.8 us -> 89.4 us (0.963)
  Pallas kernels: 89.2 us -> 87.1 us
  local copies, waits for them, and re-layouts: 3.36 us -> 2.06 us
    pallas_call x1, Pallas kernels: 89.2 us -> 87.1 us  [fused(): pl.pallas_call(functools.partial(fused_kernel, groups, places), out_shape...]
    reshape x1 -> x0, local copies, waits for them, and re-layouts: 1.29 us -> none  [fused(): norm_gain.reshape(1, width)]
where the time goes in v2:
time: 89.4 us; the launch traced here: 89.2 us
  Pallas kernels  87.1 us (97%)
  local copies, waits for them, and re-layouts  2.06 us (2%)
    pallas_call x1, Pallas kernels, fused(): pl.pallas_call(functools.partial(fused_kernel, groups, places), out_shape...  87.1 us
    unnamed x1, local copies, waits for them, and re-layouts  2.06 us

profile of v2, /device:TPU:0, one launch (start us, length us, event | category | flops | bytes accessed | tf_op | source)
XLA Modules:
  0.0 89.2 jit_solution(11089031602041792286)
XLA Ops:
  0.0 87.1 %shard_map.109 = bf16[256,1536]{1,0:T(8,128)(2,1)} custom-call(bf16[128,1536]{1,0:T(8,128)(2,1)} %bitcast.6, bf16[256,1280]{1,0:T(8,128)(2,1)} %bitcast.5, f32[1536]{0:T(1024)} %gain_ref.1, bf16[1536,256]{1,0:T(8,128)(2,1)} %wq_h.1, bf16[1536,256]{1,0:T(8,128)(2,1)} %wk_h.1, bf16[1536,768]{1,0:T(8,128)(2,1)} %wv_h.1, bf16[768,1536]{1,0:T(8,128)(2,1)} %wo_h.1, ...), custom_call_target="tpu_custom_call" | custom-call | flops 4000000000 | bytes 30000000 | tf_op jit(solution)/shard_map/pallas_call | solution.py:433
  87.1 2.1 %copy.13 = bf16[2,128,1536]{2,1,0:T(8,128)(2,1)} copy(bf16[2,128,1536]{2,1,0:T(8,128)(2,1)} %bitcast.4) | data formatting | bytes 1572864
